TPU v7x, 32 devices: a whole 2x2x4 slice. The times are simulated.
32 devices in a mesh: parts: 2 (over x), gx: 4 (over y, core), ka: 4 (over z).
Axes of the slice: x: 2, y: 2, z: 4, core: 2. Of those that a mesh axis runs over, the one named last changes fastest.
Arguments:
- bloch_modes: float32 [16, 2, 2, 3, 32, 128, 128], P(('parts', 'ka'), None, None, None, 'gx'), parts along dimension 0, may hold values from -104 to 104, as said below
- permittivity: float32 [64, 128, 128], P(('parts', 'gx')), parts along dimension 0, may hold values from 1 to 4
- bloch_phase: float32 [8], P('ka'), may hold values from -3.140625 to 3.140625
- edge_side: int32 [8, 2], P('ka'), may hold values from 0 to 1, as said below
Outputs:
- filtered_gradient: float32 [64, 128, 128], P(('parts', 'gx'), 'ka'), parts along dimension 0
- omega_squared: float32 [16, 2], P(('parts', 'ka')), parts along dimension 0
There are 2 independent parts, one for each index of `parts`. A program takes and returns all parts, laid end to end along the dimension named above; an argument that names none is the same for every part. Nothing has to cross between parts.
Inputs may be any that keep to these rules, and one draw needn't show every extreme that they name: `bloch_modes`: bloch mode fields. `edge_side`: at each k-point one of the 2 bands is the upper edge and the other the lower.
All inputs are finite; a program needn't handle non-finite values.
Results may differ from a plain program's by a relative error of at most 0.0003.
Values sent between devices are 32-bit elements; how exact they have to be, the bound alone decides.
A program may use at most 128 MiB of HBM per device.

v0:
```python
import jax
import jax.numpy as jnp
from jax import lax
from jax.sharding import PartitionSpec as P

SWEEPS = 8


filter_weight = 4.0


def passed_along(block, axis, distance):
    devices = range(lax.axis_size(axis))
    route = [((i - distance) % len(devices), i) for i in devices]
    return lax.ppermute(block, axis, route)


def with_halo(cells, sides, width):
    for axis, dim in sides:
        count = lax.axis_size(axis)
        head = lax.slice_in_dim(cells, 0, width, axis=dim)
        tail = lax.slice_in_dim(cells, cells.shape[dim] - width, cells.shape[dim], axis=dim)
        cells = jnp.concatenate(
            [
                lax.ppermute(tail, axis, [(i, (i + 1) % count) for i in range(count)]),
                cells,
                lax.ppermute(head, axis, [((i + 1) % count, i) for i in range(count)]),
            ],
            axis=dim,
        )
    return cells


def lower_z(values_in):
    zero_plane = jnp.zeros_like(values_in[..., :1])
    return jnp.concatenate([zero_plane, values_in[..., :-1]], axis=-1)


def upper_z(values_in):
    zero_plane = jnp.zeros_like(values_in[..., :1])
    return jnp.concatenate([values_in[..., 1:], zero_plane], axis=-1)


def relax_once(padded, design_source):
    center = padded[1:-1, 1:-1]
    neighbours = padded[2:, 1:-1] + padded[:-2, 1:-1] + padded[1:-1, 2:] + padded[1:-1, :-2]
    neighbours = neighbours + lower_z(center) + upper_z(center)
    return (design_source + filter_weight * neighbours) / (1.0 + 6.0 * filter_weight)


def shards(bloch_modes, permittivity, bloch_phase, edge_side):
    lower_rim = passed_along(bloch_modes[:, :, :, 1:3, -1:], "gx", 1)
    cosine = jnp.cos(bloch_phase)[:, None, None, None, None, None]
    sine_part = jnp.sin(bloch_phase)[:, None, None, None, None, None]
    real_part = lower_rim[:, :, 0]
    imag_part = lower_rim[:, :, 1]
    rotated = jnp.stack(
        [real_part * cosine + imag_part * sine_part, imag_part * cosine - real_part * sine_part],
        axis=2,
    )
    lower_rim = jnp.where(lax.axis_index("gx") == 0, rotated, lower_rim)
    field_x = bloch_modes[:, :, :, 0]
    field_y = bloch_modes[:, :, :, 1]
    field_z = bloch_modes[:, :, :, 2]
    below_y = jnp.concatenate([lower_rim[:, :, :, 0], field_y[:, :, :, :-1]], axis=3)
    below_z = jnp.concatenate([lower_rim[:, :, :, 1], field_z[:, :, :, :-1]], axis=3)
    curl_x = field_z - jnp.roll(field_z, 1, axis=4) - (field_y - lower_z(field_y))
    curl_y = field_x - lower_z(field_x) - (field_z - below_z)
    curl_z = field_y - below_y - (field_x - jnp.roll(field_x, 1, axis=4))
    squared = jnp.sum(curl_x * curl_x + curl_y * curl_y + curl_z * curl_z, axis=2)
    inverse = 1.0 / permittivity
    mode_energy = jnp.sum(squared * inverse, axis=(2, 3, 4))
    mode_norm = jnp.sum(bloch_modes * bloch_modes, axis=(2, 3, 4, 5, 6))
    mode_energy, mode_norm = lax.psum((mode_energy, mode_norm), "gx")
    omega_squared = mode_energy / mode_norm
    cell_count = (
        bloch_modes.shape[4] * lax.axis_size("gx") * bloch_modes.shape[5] * bloch_modes.shape[6]
    )
    mode_weight = -(2.0 * edge_side.astype(jnp.float32) - 1.0) * cell_count / mode_norm
    summed = jnp.sum(mode_weight[:, :, None, None, None] * squared, axis=(0, 1))
    partial_term = summed * inverse * inverse
    share_rows = permittivity.shape[1] // lax.axis_size("ka")
    whole_sum = lax.psum(partial_term, "ka")
    design_source = lax.dynamic_slice_in_dim(
        whole_sum, lax.axis_index("ka") * share_rows, share_rows, 1
    )
    density = design_source
    for sweep_index in range(SWEEPS):
        padded = with_halo(density, (("gx", 0), ("ka", 1)), 1)
        density = relax_once(padded, design_source)
    return (density, omega_squared)


def solution(mesh):
    return jax.shard_map(
        shards,
        mesh=mesh,
        in_specs=(
            P(("parts", "ka"), None, None, None, "gx", None, None),
            P(("parts", "gx"), None, None),
            P("ka"),
            P("ka", None),
        ),
        out_specs=(P(("parts", "gx"), "ka", None), P(("parts", "ka"), None)),
        check_vma=False,
    )
```

profile of v0, /device:TPU:1, one launch (start us, length us, event | category | flops | bytes accessed | tf_op | source)
XLA Modules:
  0.0 189.6 jit_solution(6374572927356271135)
XLA Ops:
  9.6 2.6 %collective-permute-start = (f32[2,2,2,2,1,128,128]{6,5,2,1,0,4,3:T(8,128)}, f32[2,2,2,2,1,128,128]{6,5,2,1,0,4,3:T(8,128)S(1)}, u32[]{:S(2)}, u32[]{:S(2)}) collective-permute-start(f32[2,2,2,2,1,128,128]{6,5,2,1,0,4,3:T(8,128)} %copy.16), channel_id=1, source_target_pairs={{12,0},{0,4},{4,8},{8,12},{13,1},{1,5},{5,9},{9,13},{14,2},{2,6},{... | collective-permute-start | bytes 3145736 | tf_op jit(solution)/shard_map/ppermute | solution.py:15
  12.3 5.6 %multiply_reduce_fusion = f32[2,2]{1,0:T(2,128)S(1)} fusion(f32[2,2,2,3,8,128,128]{6,5,4,3,2,1,0:T(8,128)} %param.4), kind=kLoop, calls=%fused_computation | loop fusion | flops 6291452 | bytes 12582928 | tf_op jit(solution)/shard_map/reduce_sum | solution.py:73
  17.9 7.7 %psum.21 = f32[2,2]{1,0:T(2,128)S(1)} all-reduce(f32[2,2]{1,0:T(2,128)S(1)} %multiply_reduce_fusion), channel_id=1, replica_groups=mesh['parts'=2,'gx'=4,'ka'=4] {'gx'}, use_global_device_ids=true, to_apply=%region_1.2 | all-reduce | flops 4 | bytes 32 | tf_op jit(solution)/shard_map/psum | solution.py:74
  25.5 9.8 %slice_bitcast_fusion = (f32[2,2,2,8,128,128]{5,4,3,2,1,0:T(8,128)}, f32[2,2,2,8,128,128]{5,4,3,2,1,0:T(8,128)S(1)}, f32[2,2,2,8,128,128]{5,4,3,2,1,0:T(8,128)}) fusion(f32[2,2,2,3,8,128,128]{6,5,4,3,2,1,0:T(8,128)} %param.4), kind=kLoop, calls=%fused_computation.14 | loop fusion | bytes 25165824 | tf_op jit(solution)/shard_map/squeeze | solution.py:62
  35.4 2.2 %slice.425 = f32[2,2,2,7,128,128]{5,4,3,2,1,0:T(8,128)} slice(f32[2,2,2,8,128,128]{5,4,3,2,1,0:T(8,128)S(1)} %get-tuple-element.5), slice={[0:2], [0:2], [0:2], [0:7], [0:128], [0:128]} | slice | bytes 7340032 | tf_op jit(solution)/shard_map/slice | solution.py:66
  39.6 4.3 %slice.427 = f32[2,2,2,7,128,128]{5,4,3,2,1,0:T(8,128)} slice(f32[2,2,2,8,128,128]{5,4,3,2,1,0:T(8,128)} %get-tuple-element.6), slice={[0:2], [0:2], [0:2], [0:7], [0:128], [0:128]} | slice | bytes 7340032 | tf_op jit(solution)/shard_map/slice | solution.py:65
  47.8 10.5 %fusion.4 = f32[2,2,8,128,128]{4,3,2,1,0:T(8,128)S(1)} fusion(f32[2,2,2,8,127,128]{5,4,3,2,1,0:T(8,128)S(1)} %bitcast.28, f32[2,2,2,8,1,128]{5,4,3,2,1,0:T(1,128)S(1)} %slice.418, f32[2,2,2,7,128,128]{5,4,3,2,1,0:T(8,128)} %slice.425, f32[2,2,2,1,128,128]{5,4,3,2,1,0:T(8,128)} %get-tuple-element.10, f32[2,2,2,7,128,128]{5,4,3,2,1,0:T(8,128)} %slice.427, ...), kind=kLoop, calls=%fused_computation.6 | loop fusion | flops 19398656 | bytes 39780352 | tf_op jit(solution)/shard_map/reduce_sum | solution.py:70
  59.9 1.9 %multiply_multiply_fusion = f32[8,128,128]{2,1,0:T(8,128)} fusion(f32[8,128,128]{2,1,0:T(8,128)S(1)} %get-tuple-element.3, f32[8,128,128]{2,1,0:T(8,128)} %param.5), kind=kLoop, calls=%fused_computation.20 | loop fusion | flops 393216 | bytes 1572864 | tf_op jit(solution)/shard_map/mul | solution.py:81
  61.9 39.0 %all-reduce.20.cloned.1.call-done = f32[8,128,128]{2,1,0:T(8,128)} async-done(((f32[8,128,128]{2,1,0:T(8,128)}), f32[8,128,128]{2,1,0:T(8,128)}) %all-reduce.20.cloned.1.call-update) | async-done | bytes 524304 | tf_op jit(solution)/shard_map/psum | solution.py:83
  105.8 2.5 %collective-permute-start.3 = (f32[10,1,128]{2,1,0:T(1,128)S(1)}, f32[10,1,128]{2,1,0:T(1,128)S(1)}, u32[]{:S(2)}, u32[]{:S(2)}) collective-permute-start(f32[10,1,128]{2,1,0:T(1,128)S(1)} %get-tuple-element.29), channel_id=1, source_target_pairs={{1,0},{2,1},{3,2},{0,3},{5,4},{6,5},{7,6},{4,7},{9,8},{10,9},{11,1... | collective-permute-start | bytes 15368 | tf_op jit(solution)/shard_map/ppermute | solution.py:27
  109.4 3.2 %collective-permute-done.4 = f32[10,1,128]{2,1,0:T(1,128)S(1)} collective-permute-done((f32[10,1,128]{2,1,0:T(1,128)S(1)}, f32[10,1,128]{2,1,0:T(1,128)S(1)}, u32[]{:S(2)}, u32[]{:S(2)}) %collective-permute-start.4) | collective-permute-done | bytes 5152 | tf_op jit(solution)/shard_map/ppermute | solution.py:25
  112.8 1.9 collective-permute-start.5
  119.9 1.9 collective-permute-done.8
  122.8 2.7 %collective-permute-start.10 = (f32[1,32,128]{2,1,0:T(8,128)S(1)}, f32[1,32,128]{2,1,0:T(8,128)S(1)}, u32[]{:S(2)}, u32[]{:S(2)}) collective-permute-start(f32[1,32,128]{2,1,0:T(8,128)S(1)} %get-tuple-element.53), channel_id=1, source_target_pairs={{0,4},{4,8},{8,12},{12,0},{1,5},{5,9},{9,13},{13,1},{2,6},{6,10},{... | collective-permute-start | bytes 49160 | tf_op jit(solution)/shard_map/ppermute | solution.py:25
  126.4 2.3 %collective-permute-done.9 = f32[1,32,128]{2,1,0:T(8,128)S(1)} collective-permute-done((f32[1,32,128]{2,1,0:T(8,128)S(1)}, f32[1,32,128]{2,1,0:T(8,128)S(1)}, u32[]{:S(2)}, u32[]{:S(2)}) %collective-permute-start.9) | collective-permute-done | bytes 16416 | tf_op jit(solution)/shard_map/ppermute | solution.py:27
  131.2 1.9 collective-permute-done.12
  140.2 1.9 collective-permute-done.16
  142.2 2.0 %collective-permute-start.17 = (f32[1,32,128]{2,1,0:T(8,128)S(1)}, f32[1,32,128]{2,1,0:T(8,128)S(1)}, u32[]{:S(2)}, u32[]{:S(2)}) collective-permute-start(f32[1,32,128]{2,1,0:T(8,128)S(1)} %get-tuple-element.46), channel_id=1, source_target_pairs={{4,0},{8,4},{12,8},{0,12},{5,1},{9,5},{13,9},{1,13},{6,2},{10,6},{... | collective-permute-start | bytes 49160 | tf_op jit(solution)/shard_map/ppermute | solution.py:27
  148.9 1.9 collective-permute-done.20
  150.9 2.2 %collective-permute-start.21 = (f32[1,32,128]{2,1,0:T(8,128)S(1)}, f32[1,32,128]{2,1,0:T(8,128)S(1)}, u32[]{:S(2)}, u32[]{:S(2)}) collective-permute-start(f32[1,32,128]{2,1,0:T(8,128)S(1)} %get-tuple-element.42), channel_id=1, source_target_pairs={{4,0},{8,4},{12,8},{0,12},{5,1},{9,5},{13,9},{1,13},{6,2},{10,6},{... | collective-permute-start | bytes 49160 | tf_op jit(solution)/shard_map/ppermute | solution.py:27
  157.9 1.9 collective-permute-done.24
  159.9 2.2 %collective-permute-start.25 = (f32[1,32,128]{2,1,0:T(8,128)S(1)}, f32[1,32,128]{2,1,0:T(8,128)S(1)}, u32[]{:S(2)}, u32[]{:S(2)}) collective-permute-start(f32[1,32,128]{2,1,0:T(8,128)S(1)} %get-tuple-element.38), channel_id=1, source_target_pairs={{4,0},{8,4},{12,8},{0,12},{5,1},{9,5},{13,9},{1,13},{6,2},{10,6},{... | collective-permute-start | bytes 49160 | tf_op jit(solution)/shard_map/ppermute | solution.py:27
  168.8 2.2 %collective-permute-start.29 = (f32[1,32,128]{2,1,0:T(8,128)S(1)}, f32[1,32,128]{2,1,0:T(8,128)S(1)}, u32[]{:S(2)}, u32[]{:S(2)}) collective-permute-start(f32[1,32,128]{2,1,0:T(8,128)S(1)} %get-tuple-element.34), channel_id=1, source_target_pairs={{4,0},{8,4},{12,8},{0,12},{5,1},{9,5},{13,9},{1,13},{6,2},{10,6},{... | collective-permute-start | bytes 49160 | tf_op jit(solution)/shard_map/ppermute | solution.py:27
  171.9 5.1 %psum.23 = f32[2,2]{1,0:T(2,128)S(1)} all-reduce(f32[2,2]{1,0:T(2,128)S(1)} %get-tuple-element.2), channel_id=1, replica_groups=mesh['parts'=2,'gx'=4,'ka'=4] {'gx'}, use_global_device_ids=true, to_apply=%region_6.7 | all-reduce | flops 4 | bytes 32 | tf_op jit(solution)/shard_map/psum | solution.py:74
  (112 shorter events, 56.0 us)
Async XLA Ops:
  7.2 93.7 %all-reduce.20.cloned.1.call-start = ((), (), s32[]{:S(2)}) async-start(), calls=%async_computation | async-start | bytes 1048576 | tf_op jit(solution)/shard_map/psum | solution.py:83
  9.6 35.2 %collective-permute-start = (f32[2,2,2,2,1,128,128]{6,5,2,1,0,4,3:T(8,128)}, f32[2,2,2,2,1,128,128]{6,5,2,1,0,4,3:T(8,128)S(1)}, u32[]{:S(2)}, u32[]{:S(2)}) collective-permute-start(f32[2,2,2,2,1,128,128]{6,5,2,1,0,4,3:T(8,128)} %copy.16), channel_id=1, source_target_pairs={{12,0},{0,4},{4,8},{8,12},{13,1},{1,5},{5,9},{9,13},{14,2},{2,6},{... | collective-permute-start | bytes 3145736 | tf_op jit(solution)/shard_map/ppermute | solution.py:15
  101.7 4.2 %collective-permute-start.1 = (f32[1,32,128]{2,1,0:T(8,128)S(1)}, f32[1,32,128]{2,1,0:T(8,128)S(1)}, u32[]{:S(2)}, u32[]{:S(2)}) collective-permute-start(f32[1,32,128]{2,1,0:T(8,128)S(1)} %get-tuple-element.14), channel_id=1, source_target_pairs={{4,0},{8,4},{12,8},{0,12},{5,1},{9,5},{13,9},{1,13},{6,2},{10,6},{... | collective-permute-start | bytes 49160 | tf_op jit(solution)/shard_map/ppermute | solution.py:27
  105.8 3.6 %collective-permute-start.3 = (f32[10,1,128]{2,1,0:T(1,128)S(1)}, f32[10,1,128]{2,1,0:T(1,128)S(1)}, u32[]{:S(2)}, u32[]{:S(2)}) collective-permute-start(f32[10,1,128]{2,1,0:T(1,128)S(1)} %get-tuple-element.29), channel_id=1, source_target_pairs={{1,0},{2,1},{3,2},{0,3},{5,4},{6,5},{7,6},{4,7},{9,8},{10,9},{11,1... | collective-permute-start | bytes 15368 | tf_op jit(solution)/shard_map/ppermute | solution.py:27
  108.4 4.3 %collective-permute-start.4 = (f32[10,1,128]{2,1,0:T(1,128)S(1)}, f32[10,1,128]{2,1,0:T(1,128)S(1)}, u32[]{:S(2)}, u32[]{:S(2)}) collective-permute-start(f32[10,1,128]{2,1,0:T(1,128)S(1)} %get-tuple-element.30), channel_id=1, source_target_pairs={{0,1},{1,2},{2,3},{3,0},{4,5},{5,6},{6,7},{7,4},{8,9},{9,10},{10,1... | collective-permute-start | bytes 15368 | tf_op jit(solution)/shard_map/ppermute | solution.py:25
  112.8 4.6 %collective-permute-start.5 = (f32[1,32,128]{2,1,0:T(8,128)S(1)}, f32[1,32,128]{2,1,0:T(8,128)S(1)}, u32[]{:S(2)}, u32[]{:S(2)}) collective-permute-start(f32[1,32,128]{2,1,0:T(8,128)S(1)} %get-tuple-element.58), channel_id=1, source_target_pairs={{4,0},{8,4},{12,8},{0,12},{5,1},{9,5},{13,9},{1,13},{6,2},{10,6},{... | collective-permute-start | bytes 49160 | tf_op jit(solution)/shard_map/ppermute | solution.py:27
  114.6 2.8 %collective-permute-start.6 = (f32[1,32,128]{2,1,0:T(8,128)S(1)}, f32[1,32,128]{2,1,0:T(8,128)S(1)}, u32[]{:S(2)}, u32[]{:S(2)}) collective-permute-start(f32[1,32,128]{2,1,0:T(8,128)S(1)} %get-tuple-element.57), channel_id=1, source_target_pairs={{0,4},{4,8},{8,12},{12,0},{1,5},{5,9},{9,13},{13,1},{2,6},{6,10},{... | collective-permute-start | bytes 49160 | tf_op jit(solution)/shard_map/ppermute | solution.py:25
  117.4 2.5 %collective-permute-start.7 = (f32[10,1,128]{2,1,0:T(1,128)S(1)}, f32[10,1,128]{2,1,0:T(1,128)S(1)}, u32[]{:S(2)}, u32[]{:S(2)}) collective-permute-start(f32[10,1,128]{2,1,0:T(1,128)S(1)} %get-tuple-element.27), channel_id=1, source_target_pairs={{1,0},{2,1},{3,2},{0,3},{5,4},{6,5},{7,6},{4,7},{9,8},{10,9},{11,1... | collective-permute-start | bytes 15368 | tf_op jit(solution)/shard_map/ppermute | solution.py:27
  117.5 4.3 %collective-permute-start.8 = (f32[10,1,128]{2,1,0:T(1,128)S(1)}, f32[10,1,128]{2,1,0:T(1,128)S(1)}, u32[]{:S(2)}, u32[]{:S(2)}) collective-permute-start(f32[10,1,128]{2,1,0:T(1,128)S(1)} %get-tuple-element.28), channel_id=1, source_target_pairs={{0,1},{1,2},{2,3},{3,0},{4,5},{5,6},{6,7},{7,4},{8,9},{9,10},{10,1... | collective-permute-start | bytes 15368 | tf_op jit(solution)/shard_map/ppermute | solution.py:25
  122.8 3.5 %collective-permute-start.10 = (f32[1,32,128]{2,1,0:T(8,128)S(1)}, f32[1,32,128]{2,1,0:T(8,128)S(1)}, u32[]{:S(2)}, u32[]{:S(2)}) collective-permute-start(f32[1,32,128]{2,1,0:T(8,128)S(1)} %get-tuple-element.53), channel_id=1, source_target_pairs={{0,4},{4,8},{8,12},{12,0},{1,5},{5,9},{9,13},{13,1},{2,6},{6,10},{... | collective-permute-start | bytes 49160 | tf_op jit(solution)/shard_map/ppermute | solution.py:25
  125.5 3.2 %collective-permute-start.9 = (f32[1,32,128]{2,1,0:T(8,128)S(1)}, f32[1,32,128]{2,1,0:T(8,128)S(1)}, u32[]{:S(2)}, u32[]{:S(2)}) collective-permute-start(f32[1,32,128]{2,1,0:T(8,128)S(1)} %get-tuple-element.54), channel_id=1, source_target_pairs={{4,0},{8,4},{12,8},{0,12},{5,1},{9,5},{13,9},{1,13},{6,2},{10,6},{... | collective-permute-start | bytes 49160 | tf_op jit(solution)/shard_map/ppermute | solution.py:27
  128.7 4.3 %collective-permute-start.12 = (f32[10,1,128]{2,1,0:T(1,128)S(1)}, f32[10,1,128]{2,1,0:T(1,128)S(1)}, u32[]{:S(2)}, u32[]{:S(2)}) collective-permute-start(f32[10,1,128]{2,1,0:T(1,128)S(1)} %get-tuple-element.26), channel_id=1, source_target_pairs={{0,1},{1,2},{2,3},{3,0},{4,5},{5,6},{6,7},{7,4},{8,9},{9,10},{10,1... | collective-permute-start | bytes 15368 | tf_op jit(solution)/shard_map/ppermute | solution.py:25
  134.1 3.6 %collective-permute-start.13 = (f32[1,32,128]{2,1,0:T(8,128)S(1)}, f32[1,32,128]{2,1,0:T(8,128)S(1)}, u32[]{:S(2)}, u32[]{:S(2)}) collective-permute-start(f32[1,32,128]{2,1,0:T(8,128)S(1)} %get-tuple-element.50), channel_id=1, source_target_pairs={{4,0},{8,4},{12,8},{0,12},{5,1},{9,5},{13,9},{1,13},{6,2},{10,6},{... | collective-permute-start | bytes 49160 | tf_op jit(solution)/shard_map/ppermute | solution.py:27
  134.4 3.3 %collective-permute-start.14 = (f32[1,32,128]{2,1,0:T(8,128)S(1)}, f32[1,32,128]{2,1,0:T(8,128)S(1)}, u32[]{:S(2)}, u32[]{:S(2)}) collective-permute-start(f32[1,32,128]{2,1,0:T(8,128)S(1)} %get-tuple-element.49), channel_id=1, source_target_pairs={{0,4},{4,8},{8,12},{12,0},{1,5},{5,9},{9,13},{13,1},{2,6},{6,10},{... | collective-permute-start | bytes 49160 | tf_op jit(solution)/shard_map/ppermute | solution.py:25
  137.7 4.3 %collective-permute-start.16 = (f32[10,1,128]{2,1,0:T(1,128)S(1)}, f32[10,1,128]{2,1,0:T(1,128)S(1)}, u32[]{:S(2)}, u32[]{:S(2)}) collective-permute-start(f32[10,1,128]{2,1,0:T(1,128)S(1)} %get-tuple-element.24), channel_id=1, source_target_pairs={{0,1},{1,2},{2,3},{3,0},{4,5},{5,6},{6,7},{7,4},{8,9},{9,10},{10,1... | collective-permute-start | bytes 15368 | tf_op jit(solution)/shard_map/ppermute | solution.py:25
  142.2 4.2 %collective-permute-start.17 = (f32[1,32,128]{2,1,0:T(8,128)S(1)}, f32[1,32,128]{2,1,0:T(8,128)S(1)}, u32[]{:S(2)}, u32[]{:S(2)}) collective-permute-start(f32[1,32,128]{2,1,0:T(8,128)S(1)} %get-tuple-element.46), channel_id=1, source_target_pairs={{4,0},{8,4},{12,8},{0,12},{5,1},{9,5},{13,9},{1,13},{6,2},{10,6},{... | collective-permute-start | bytes 49160 | tf_op jit(solution)/shard_map/ppermute | solution.py:27
  146.5 4.3 %collective-permute-start.20 = (f32[10,1,128]{2,1,0:T(1,128)S(1)}, f32[10,1,128]{2,1,0:T(1,128)S(1)}, u32[]{:S(2)}, u32[]{:S(2)}) collective-permute-start(f32[10,1,128]{2,1,0:T(1,128)S(1)} %get-tuple-element.22), channel_id=1, source_target_pairs={{0,1},{1,2},{2,3},{3,0},{4,5},{5,6},{6,7},{7,4},{8,9},{9,10},{10,1... | collective-permute-start | bytes 15368 | tf_op jit(solution)/shard_map/ppermute | solution.py:25
  150.9 4.4 %collective-permute-start.21 = (f32[1,32,128]{2,1,0:T(8,128)S(1)}, f32[1,32,128]{2,1,0:T(8,128)S(1)}, u32[]{:S(2)}, u32[]{:S(2)}) collective-permute-start(f32[1,32,128]{2,1,0:T(8,128)S(1)} %get-tuple-element.42), channel_id=1, source_target_pairs={{4,0},{8,4},{12,8},{0,12},{5,1},{9,5},{13,9},{1,13},{6,2},{10,6},{... | collective-permute-start | bytes 49160 | tf_op jit(solution)/shard_map/ppermute | solution.py:27
  155.4 4.3 %collective-permute-start.24 = (f32[10,1,128]{2,1,0:T(1,128)S(1)}, f32[10,1,128]{2,1,0:T(1,128)S(1)}, u32[]{:S(2)}, u32[]{:S(2)}) collective-permute-start(f32[10,1,128]{2,1,0:T(1,128)S(1)} %get-tuple-element.20), channel_id=1, source_target_pairs={{0,1},{1,2},{2,3},{3,0},{4,5},{5,6},{6,7},{7,4},{8,9},{9,10},{10,1... | collective-permute-start | bytes 15368 | tf_op jit(solution)/shard_map/ppermute | solution.py:25
  159.9 4.4 %collective-permute-start.25 = (f32[1,32,128]{2,1,0:T(8,128)S(1)}, f32[1,32,128]{2,1,0:T(8,128)S(1)}, u32[]{:S(2)}, u32[]{:S(2)}) collective-permute-start(f32[1,32,128]{2,1,0:T(8,128)S(1)} %get-tuple-element.38), channel_id=1, source_target_pairs={{4,0},{8,4},{12,8},{0,12},{5,1},{9,5},{13,9},{1,13},{6,2},{10,6},{... | collective-permute-start | bytes 49160 | tf_op jit(solution)/shard_map/ppermute | solution.py:27
  164.4 4.3 %collective-permute-start.28 = (f32[10,1,128]{2,1,0:T(1,128)S(1)}, f32[10,1,128]{2,1,0:T(1,128)S(1)}, u32[]{:S(2)}, u32[]{:S(2)}) collective-permute-start(f32[10,1,128]{2,1,0:T(1,128)S(1)} %get-tuple-element.18), channel_id=1, source_target_pairs={{0,1},{1,2},{2,3},{3,0},{4,5},{5,6},{6,7},{7,4},{8,9},{9,10},{10,1... | collective-permute-start | bytes 15368 | tf_op jit(solution)/shard_map/ppermute | solution.py:25
  168.8 8.7 %collective-permute-start.29 = (f32[1,32,128]{2,1,0:T(8,128)S(1)}, f32[1,32,128]{2,1,0:T(8,128)S(1)}, u32[]{:S(2)}, u32[]{:S(2)}) collective-permute-start(f32[1,32,128]{2,1,0:T(8,128)S(1)} %get-tuple-element.34), channel_id=1, source_target_pairs={{4,0},{8,4},{12,8},{0,12},{5,1},{9,5},{13,9},{1,13},{6,2},{10,6},{... | collective-permute-start | bytes 49160 | tf_op jit(solution)/shard_map/ppermute | solution.py:27
  171.1 6.5 %collective-permute-start.30 = (f32[1,32,128]{2,1,0:T(8,128)S(1)}, f32[1,32,128]{2,1,0:T(8,128)S(1)}, u32[]{:S(2)}, u32[]{:S(2)}) collective-permute-start(f32[1,32,128]{2,1,0:T(8,128)S(1)} %get-tuple-element.33), channel_id=1, source_target_pairs={{0,4},{4,8},{8,12},{12,0},{1,5},{5,9},{9,13},{13,1},{2,6},{6,10},{... | collective-permute-start | bytes 49160 | tf_op jit(solution)/shard_map/ppermute | solution.py:25
  177.7 4.3 %collective-permute-start.32 = (f32[10,1,128]{2,1,0:T(1,128)S(1)}, f32[10,1,128]{2,1,0:T(1,128)S(1)}, u32[]{:S(2)}, u32[]{:S(2)}) collective-permute-start(f32[10,1,128]{2,1,0:T(1,128)S(1)} %get-tuple-element.16), channel_id=1, source_target_pairs={{0,1},{1,2},{2,3},{3,0},{4,5},{5,6},{6,7},{7,4},{8,9},{9,10},{10,1... | collective-permute-start | bytes 15368 | tf_op jit(solution)/shard_map/ppermute | solution.py:25
  (17 other events, 91.1 us)
Sparse Core Ops, SparseCore 0:
  62.0 38.8 all-reduce.19
where the time goes:
time: 193 us; the launch traced here: 190 us
  waiting for transfers between devices  72.8 us (38%)
  starting transfers between devices  38 us (20%)
  local copies, waits for them, and re-layouts  26.8 us (14%)
  other arithmetic  24.9 us (13%)
  between operations  14.4 us (7%)
  blocking collectives  12.8 us (7%)
    psum x1, waiting for transfers between devices, shards(): whole_sum = lax.psum(partial_term, 'ka')  39 us
    ppermute x16, starting transfers between devices, with_halo(): lax.ppermute(tail, axis, [(i, (i + 1) % count) for i in range(count)])  19.8 us
    ppermute x16, waiting for transfers between devices, with_halo(): lax.ppermute(tail, axis, [(i, (i + 1) % count) for i in range(count)])  17.1 us
    ppermute x16, waiting for transfers between devices, with_halo(): lax.ppermute(head, axis, [((i + 1) % count, i) for i in range(count)])  16.7 us
    ppermute x16, starting transfers between devices, with_halo(): lax.ppermute(head, axis, [((i + 1) % count, i) for i in range(count)])  15.5 us
    psum x2, blocking collectives, shards(): mode_energy, mode_norm = lax.psum((mode_energy, mode_norm), 'gx')  12.8 us
    reduce_sum x1, other arithmetic, shards(): jnp.sum(curl_x * curl_x + curl_y * curl_y + curl_z * curl_z, axis=2)  10.5 us
    squeeze x1, local copies, waits for them, and re-layouts, shards(): field_x = bloch_modes[:, :, :, 0]  9.8 us
  transfers between devices with their start and end apart: 34, of which 24 were waited for; matrix products, arithmetic and copies ran while one was open for 14% of the time, Pallas kernels for 0%

commit v1 on v0

v1 whole, which is shorter than its diff:
```python
import functools

import jax
import jax.numpy as jnp
from jax import lax
from jax.experimental import pallas as pl
from jax.experimental.pallas import tpu as pltpu
from jax.sharding import PartitionSpec as P

SWEEPS = 8
FILTER_WEIGHT = 4.0
W = SWEEPS
MESH = pl.DeviceIdType.MESH
SIDES = tuple((dx, dy) for dx in (-1, 0, 1) for dy in (-1, 0, 1) if (dx, dy) != (0, 0))


def kernel(n_gx, n_ka, modes, perm_hbm, phase, edge, out, omega,
           fields, halo, perm, inv, part, recv, gpad, dens, norm_msg, energy_msg, weight, energy, rot,
           load_sem, perm_sem, halo_send, halo_recv, norm_send, norm_recv, energy_send, energy_recv,
           red_send, red_recv, side_send, side_recv):
    K, B, _, _, PL, NY, NZ = fields.shape
    R = NY // n_ka
    M = K * B
    gx = lax.axis_index("gx")
    ka = lax.axis_index("ka")

    def gx_at(d):
        return lax.rem(gx + d + n_gx, n_gx)

    def ka_at(d):
        return lax.rem(ka + d + n_ka, n_ka)

    loads = [pltpu.make_async_copy(modes.at[m // B, m % B], fields.at[m // B, m % B], load_sem.at[m]) for m in range(M)]
    for c in loads:
        c.start()
    perm_load = pltpu.make_async_copy(perm_hbm, perm, perm_sem)
    perm_load.start()

    barrier = pltpu.get_barrier_semaphore()
    partners = [(d, 0) for d in range(1, n_gx)] + [(0, d) for d in range(1, n_ka)] + [s for s in SIDES if 0 not in s]
    for dx, dy in partners:
        pl.semaphore_signal(barrier, inc=1, device_id={"gx": gx_at(dx), "ka": ka_at(dy)}, device_id_type=MESH)
    pl.semaphore_wait(barrier, len(partners))

    halos = [
        pltpu.make_async_remote_copy(
            src_ref=modes.at[m // B, m % B, :, 1:3, PL - 1], dst_ref=halo.at[m // B, m % B],
            send_sem=halo_send.at[m], recv_sem=halo_recv.at[m],
            device_id={"gx": gx_at(1)}, device_id_type=MESH)
        for m in range(M)
    ]
    for c in halos:
        c.start()

    norm_msg[gx] = jnp.zeros((8, NZ), jnp.float32)
    for m in range(M):
        loads[m].wait()

        def norm_step(p, acc, m=m):
            for ri in range(2):
                for comp in range(3):
                    x = fields[m // B, m % B, ri, comp, p]
                    acc = acc + jnp.sum((x * x).reshape(NY // 8, 8, NZ), axis=0)
            return acc

        acc = lax.fori_loop(0, PL, norm_step, jnp.zeros((8, NZ), jnp.float32))
        norm_msg[gx, m:m + 1] = jnp.sum(acc, axis=0, keepdims=True)

    def exchange(msg, send, recv_sems):
        copies = []
        for d in range(1, n_gx):
            copies.append(pltpu.make_async_remote_copy(
                src_ref=msg.at[gx], dst_ref=msg.at[gx], send_sem=send.at[d], recv_sem=recv_sems.at[gx],
                device_id={"gx": gx_at(d)}, device_id_type=MESH))
        for c in copies:
            c.start()
        return copies

    def gather(msg, send, recv_sems):
        for d in range(1, n_gx):
            src = gx_at(d)
            pltpu.make_async_remote_copy(
                src_ref=msg.at[src], dst_ref=msg.at[src], send_sem=send.at[d], recv_sem=recv_sems.at[src],
                device_id={"gx": src}, device_id_type=MESH).wait_recv()
        total = msg[0]
        for i in range(1, n_gx):
            total = total + msg[i]
        return jnp.broadcast_to(jnp.sum(total, axis=1, keepdims=True), (8, NZ))

    norm_copies = exchange(norm_msg, norm_send, norm_recv)

    perm_load.wait()

    def inverse_step(p, carry):
        inv[p] = 1.0 / perm[p]
        return carry

    lax.fori_loop(0, PL, inverse_step, 0)
    for k in range(K):
        angle = jnp.full((8, NZ), phase[k], jnp.float32)
        rot[k, 0] = jnp.where(gx == 0, jnp.cos(angle), 1.0)
        rot[k, 1] = jnp.where(gx == 0, jnp.sin(angle), 0.0)
    energy[...] = jnp.zeros_like(energy)

    norms = gather(norm_msg, norm_send, norm_recv)
    cells = float(n_gx * PL * NY * NZ)
    for m in range(M):
        sign = 1.0 - 2.0 * edge[m // B, m % B].astype(jnp.float32)
        weight[m] = jnp.broadcast_to(sign * cells / norms[m:m + 1], (8, NZ))

    first_lane = lax.broadcasted_iota(jnp.int32, (R, NZ), 1) == 0
    last_lane = lax.broadcasted_iota(jnp.int32, (W + R + W, NZ), 1) == NZ - 1
    first_lane_wide = lax.broadcasted_iota(jnp.int32, (W + R + W, NZ), 1) == 0

    def red_copy(p, c):
        return pltpu.make_async_remote_copy(
            src_ref=part.at[c, p], dst_ref=recv.at[ka, p], send_sem=red_send.at[c, p], recv_sem=red_recv.at[ka, p],
            device_id={"ka": c}, device_id_type=MESH)

    def chunk(p, c, first):
        r0 = pl.multiple_of(c * R, R)
        rows = pl.ds(r0, R)
        before = pl.ds(pl.multiple_of(lax.rem(r0 + NY - 8, NY), 8), 8)
        inverse = inv[p, rows]
        total = jnp.zeros((R, NZ), jnp.float32)
        tile = lambda a: jnp.concatenate([a] * (R // 8), axis=0)
        for m in range(M):
            k, b = m // B, m % B
            square = None
            if first:
                cosine, sine = tile(rot[k, 0]), tile(rot[k, 1])
                old = [[halo[k, b, ri, comp, rows] for comp in range(2)] for ri in range(2)]
                low = [[old[0][comp] * cosine + old[1][comp] * sine for comp in range(2)],
                       [old[1][comp] * cosine - old[0][comp] * sine for comp in range(2)]]
            for ri in range(2):
                hx, hy, hz = [fields[k, b, ri, comp, p, rows] for comp in range(3)]
                if first:
                    hy_low, hz_low = low[ri]
                else:
                    hy_low, hz_low = [fields[k, b, ri, comp, p - 1, rows] for comp in (1, 2)]

                def below(comp, h):
                    both = jnp.concatenate([fields[k, b, ri, comp, p, before], h], axis=0)
                    return pltpu.roll(both, 1, 0)[8:]

                def lower(h):
                    return jnp.where(first_lane, 0.0, pltpu.roll(h, 1, 1))

                curl_x = (hz - below(2, hz)) - (hy - lower(hy))
                curl_y = (hx - lower(hx)) - (hz - hz_low)
                curl_z = (hy - hy_low) - (hx - below(0, hx))
                value = curl_x * curl_x + curl_y * curl_y + curl_z * curl_z
                square = value if square is None else square + value
            energy[m] += jnp.sum((square * inverse).reshape(R // 8, 8, NZ), axis=0)
            total = total + tile(weight[m]) * square
        part[c, p] = total * inverse * inverse

        @pl.when(c != ka)
        def _():
            red_copy(p, c).start()

    def stage_a(i, carry):
        chunk(1 + i // n_ka, lax.rem(i, n_ka), False)
        return carry

    lax.fori_loop(0, (PL - 1) * n_ka, stage_a, 0)

    for c in halos:
        c.wait_recv()

    def stage_b(c, carry):
        chunk(0, c, True)
        return carry

    lax.fori_loop(0, n_ka, stage_b, 0)

    energy_msg[gx] = jnp.zeros((8, NZ), jnp.float32)
    for m in range(M):
        energy_msg[gx, m:m + 1] = jnp.sum(energy[m], axis=0, keepdims=True)
    energy_copies = exchange(energy_msg, energy_send, energy_recv)

    def gathered(p):
        total = part[ka, p]
        for d in range(1, n_ka):
            src = ka_at(d)
            pltpu.make_async_remote_copy(
                src_ref=part.at[src, p], dst_ref=recv.at[src, p], send_sem=red_send.at[src, p],
                recv_sem=red_recv.at[src, p], device_id={"ka": src}, device_id_type=MESH).wait_recv()
            total = total + recv[src, p]
        gpad[W + p, W:W + R] = total

    def side_copies(stage, p0, planes):
        copies = []
        for i, (dx, dy) in enumerate(SIDES):
            rows = R if dy == 0 else W
            src_row = {0: W, 1: R, -1: W}[dy]
            dst_row = {0: W, 1: 0, -1: W + R}[dy]
            copies.append(pltpu.make_async_remote_copy(
                src_ref=gpad.at[pl.ds(W + p0, planes), pl.ds(src_row, rows)],
                dst_ref=gpad.at[pl.ds(W - dx * PL + p0, planes), pl.ds(dst_row, rows)],
                send_sem=side_send.at[stage, i], recv_sem=side_recv.at[stage, i],
                device_id={"gx": gx_at(dx), "ka": ka_at(dy)}, device_id_type=MESH))
        for c in copies:
            c.start()
        return copies

    def gather_step(p, carry):
        gathered(p)
        return carry

    lax.fori_loop(1, PL, gather_step, 0)
    sides = side_copies(0, 1, PL - 1)
    gathered(0)
    sides += side_copies(1, 0, 1)
    for c in sides:
        c.wait_recv()

    scale = 1.0 / (1.0 + 6.0 * FILTER_WEIGHT)
    for sweep in range(1, SWEEPS + 1):
        source = gpad if sweep == 1 else dens.at[sweep % 2]
        target = dens.at[(sweep + 1) % 2]

        def relax(p, carry, sweep=sweep, source=source, target=target):
            under, center = carry
            over = source[p + 1]
            near = under + over + pltpu.roll(center, 1, 0) + pltpu.roll(center, W + R + W - 1, 0)
            near = near + jnp.where(first_lane_wide, 0.0, pltpu.roll(center, 1, 1))
            near = near + jnp.where(last_lane, 0.0, pltpu.roll(center, NZ - 1, 1))
            value = (gpad[p] + FILTER_WEIGHT * near) * scale
            if sweep == SWEEPS:
                out[p - W] = value[W:W + R]
            else:
                target[p] = value
            return center, over

        lax.fori_loop(sweep, 2 * W + PL - sweep, relax, (source[sweep - 1], source[sweep]))

    energies = gather(energy_msg, energy_send, energy_recv)
    ratio = energies / norms
    for m in range(M):
        omega[m // B, m % B] = ratio[m, 0]

    for c in halos + norm_copies + energy_copies + sides:
        c.wait_send()

    def sent(p, carry):
        for d in range(1, n_ka):
            red_copy(p, ka_at(d)).wait_send()
        return carry

    lax.fori_loop(0, PL, sent, 0)


def shards(n_gx, n_ka, bloch_modes, permittivity, bloch_phase, edge_side):
    K, B, _, _, PL, NY, NZ = bloch_modes.shape
    R = NY // n_ka
    assert PL == W and R >= W
    M = K * B
    f32 = jnp.float32
    dma = pltpu.SemaphoreType.DMA
    return pl.pallas_call(
        functools.partial(kernel, n_gx, n_ka),
        out_shape=(jax.ShapeDtypeStruct((PL, R, NZ), f32), jax.ShapeDtypeStruct((K, B), f32)),
        in_specs=[pl.BlockSpec(memory_space=pl.ANY), pl.BlockSpec(memory_space=pl.ANY),
                  pl.BlockSpec(memory_space=pltpu.SMEM), pl.BlockSpec(memory_space=pltpu.SMEM)],
        out_specs=(pl.BlockSpec(memory_space=pltpu.VMEM), pl.BlockSpec(memory_space=pltpu.SMEM)),
        scratch_shapes=[
            pltpu.VMEM((K, B, 2, 3, PL, NY, NZ), f32),
            pltpu.VMEM((K, B, 2, 2, NY, NZ), f32),
            pltpu.VMEM((PL, NY, NZ), f32),
            pltpu.VMEM((PL, NY, NZ), f32),
            pltpu.VMEM((n_ka, PL, R, NZ), f32),
            pltpu.VMEM((n_ka, PL, R, NZ), f32),
            pltpu.VMEM((PL + 2 * W, R + 2 * W, NZ), f32),
            pltpu.VMEM((2, PL + 2 * W, R + 2 * W, NZ), f32),
            pltpu.VMEM((n_gx, 8, NZ), f32),
            pltpu.VMEM((n_gx, 8, NZ), f32),
            pltpu.VMEM((M, 8, NZ), f32),
            pltpu.VMEM((M, 8, NZ), f32),
            pltpu.VMEM((K, 2, 8, NZ), f32),
            dma((M,)), dma, dma((M,)), dma((M,)),
            dma((n_gx,)), dma((n_gx,)), dma((n_gx,)), dma((n_gx,)),
            dma((n_ka, PL)), dma((n_ka, PL)), dma((2, len(SIDES))), dma((2, len(SIDES))),
        ],
        compiler_params=pltpu.CompilerParams(
            collective_id=0, has_side_effects=True, vmem_limit_bytes=48 * 1024 * 1024),
    )(bloch_modes, permittivity, bloch_phase, edge_side)


def solution(mesh):
    return jax.shard_map(
        functools.partial(shards, mesh.shape["gx"], mesh.shape["ka"]),
        mesh=mesh,
        in_specs=(
            P(("parts", "ka"), None, None, None, "gx", None, None),
            P(("parts", "gx"), None, None),
            P("ka"),
            P("ka", None),
        ),
        out_specs=(P(("parts", "gx"), "ka", None), P(("parts", "ka"), None)),
        check_vma=False,
    )
```

time: 193 us -> 55.5 us (0.29); the launches traced: 190 us -> 55.1 us
  waiting for transfers between devices: 72.8 us -> 0 us
  Pallas kernels: 0 us -> 50.9 us
  starting transfers between devices: 38 us -> 0 us
  other arithmetic: 24.9 us -> 0 us
  local copies, waits for them, and re-layouts: 26.8 us -> 3.59 us
  between operations: 14.4 us -> 0.65 us
  blocking collectives: 12.8 us -> 0 us
    pallas_call x0 -> x1, Pallas kernels: none -> 50.9 us  [shards(): pl.pallas_call(functools.partial(kernel, n_gx, n_ka), out_shape=(jax.Shap...]
    psum x1 -> x0, waiting for transfers between devices: 39 us -> none  [shards(): whole_sum = lax.psum(partial_term, 'ka')]
    ppermute x33 -> x0, starting transfers between devices: 37.9 us -> none  [the longest x16 19.8 us: with_halo(): lax.ppermute(tail, axis, [(i, (i + 1) % count) for i in range(count)])]
    ppermute x33 -> x0, waiting for transfers between devices: 33.8 us -> none  [the longest x16 17.1 us: with_halo(): lax.ppermute(tail, axis, [(i, (i + 1) % count) for i in range(count)])]
    reduce_sum x3 -> x0, other arithmetic: 17.7 us -> none  [the longest x1 10.5 us: shards(): jnp.sum(curl_x * curl_x + curl_y * curl_y + curl_z * curl_z, axis=2)]
    psum x2 -> x0, blocking collectives: 12.8 us -> none  [shards(): mode_energy, mode_norm = lax.psum((mode_energy, mode_norm), 'gx')]
    slice x21 -> x0, local copies, waits for them, and re-layouts: 11.3 us -> none  [the longest x1 4.26 us: shards(): field_y[:, :, :, :-1]]
    squeeze x2 -> x0, local copies, waits for them, and re-layouts: 10.7 us -> none  [the longest x1 9.8 us: shards(): field_x = bloch_modes[:, :, :, 0]]
  transfers between devices with their start and end apart: 34 -> 0, of which waited for: 24 -> 0; matrix products, arithmetic and copies ran while one was open for 14% -> 0% of each run, Pallas kernels for 0% -> 0%
where the time goes in v1:
time: 55.5 us; the launch traced here: 55.1 us
  Pallas kernels  50.9 us (92%)
  local copies, waits for them, and re-layouts  3.59 us (6%)
  between operations  0.65 us (1%)
    pallas_call x1, Pallas kernels, shards(): pl.pallas_call(functools.partial(kernel, n_gx, n_ka), out_shape=(jax.Shap...  50.9 us
    unnamed x8, local copies, waits for them, and re-layouts  3.59 us

profile of v1, /device:TPU:1, one launch (start us, length us, event | category | flops | bytes accessed | tf_op | source)
XLA Modules:
  0.0 55.1 jit_solution(15146852196610436008)
XLA Ops:
  0.6 0.0 copy-start
  0.6 1.0 %copy-done = f32[8,128,128]{2,1,0:T(8,128)S(1)} copy-done((f32[8,128,128]{2,1,0:T(8,128)S(1)}, f32[8,128,128]{2,1,0:T(8,128)}, u32[]{:S(2)}) %copy-start) | copy-done | bytes 524312
  1.7 0.0 copy-start.1
  1.7 0.7 %copy-done.1 = s32[2,2]{1,0:T(2,128)S(1)} copy-done((s32[2,2]{1,0:T(2,128)S(1)}, s32[2,2]{1,0:T(2,128)}, u32[]{:S(2)}) %copy-start.1) | copy-done | bytes 40
  2.4 0.0 copy-start.2
  2.4 0.7 %copy-done.2 = f32[2]{0:T(128)S(1)} copy-done((f32[2]{0:T(128)S(1)}, f32[2]{0:T(128)}, u32[]{:S(2)}) %copy-start.2) | copy-done | bytes 32
  3.0 50.9 %shard_map.59 = (f32[8,32,128]{2,1,0:T(8,128)S(1)}, f32[2,2]{1,0:T(2,128)S(1)}) custom-call(f32[2,2,2,3,8,128,128]{6,5,4,3,2,1,0:T(8,128)} %modes.1, f32[8,128,128]{2,1,0:T(8,128)S(1)} %copy-done, f32[2]{0:T(128)S(1)} %copy-done.2, s32[2,2]{1,0:T(2,128)S(1)} %copy-done.1), custom_call_target="tpu_custom_call" | custom-call | tf_op jit(solution)/shard_map/pallas_call | solution.py:261
  53.9 0.7 %copy.8 = f32[8,32,128]{2,1,0:T(8,128)} copy(f32[8,32,128]{2,1,0:T(8,128)S(1)} %get-tuple-element.4) | data formatting | bytes 262144
  54.5 0.6 %copy.9 = f32[2,2]{1,0:T(2,128)} copy(f32[2,2]{1,0:T(2,128)S(1)} %get-tuple-element.5) | data formatting | bytes 32
Async XLA Ops:
  0.6 1.0 %copy-start = (f32[8,128,128]{2,1,0:T(8,128)S(1)}, f32[8,128,128]{2,1,0:T(8,128)}, u32[]{:S(2)}) copy-start(f32[8,128,128]{2,1,0:T(8,128)} %perm_hbm.1) | copy-start | bytes 1572868
  1.7 0.7 %copy-start.1 = (s32[2,2]{1,0:T(2,128)S(1)}, s32[2,2]{1,0:T(2,128)}, u32[]{:S(2)}) copy-start(s32[2,2]{1,0:T(2,128)} %edge.1) | copy-start | bytes 52
  2.4 0.7 %copy-start.2 = (f32[2]{0:T(128)S(1)}, f32[2]{0:T(128)}, u32[]{:S(2)}) copy-start(f32[2]{0:T(128)} %phase.1) | copy-start | bytes 28

commit v2 on v1

--- a/solution.py
+++ b/solution.py
@@ -11,12 +11,12 @@
 FILTER_WEIGHT = 4.0
 W = SWEEPS
 MESH = pl.DeviceIdType.MESH
-SIDES = tuple((dx, dy) for dx in (-1, 0, 1) for dy in (-1, 0, 1) if (dx, dy) != (0, 0))
-
-
-def kernel(n_gx, n_ka, modes, perm_hbm, phase, edge, out, omega,
-           fields, halo, perm, inv, part, recv, gpad, dens, norm_msg, energy_msg, weight, energy, rot,
-           load_sem, perm_sem, halo_send, halo_recv, norm_send, norm_recv, energy_send, energy_recv,
+PLANES = 2
+
+
+def kernel(n_gx, n_ka, modes, perm_hbm, phase_hbm, edge_hbm, out_hbm, omega_hbm,
+           fields, halo, perm, inv, part, recv, gpad, dens_a, dens_b, out, omega, phase, edge, norm_msg, energy_msg, weight, energy, rot,
+           load_sem, perm_sem, small_sem, out_sem, halo_send, halo_recv, norm_send, norm_recv, energy_send, energy_recv,
            red_send, red_recv, side_send, side_recv):
     K, B, _, _, PL, NY, NZ = fields.shape
     R = NY // n_ka
@@ -35,9 +35,13 @@
         c.start()
     perm_load = pltpu.make_async_copy(perm_hbm, perm, perm_sem)
     perm_load.start()
+    small_loads = [pltpu.make_async_copy(phase_hbm, phase, small_sem.at[0]),
+                   pltpu.make_async_copy(edge_hbm, edge, small_sem.at[1])]
+    for c in small_loads:
+        c.start()
 
     barrier = pltpu.get_barrier_semaphore()
-    partners = [(d, 0) for d in range(1, n_gx)] + [(0, d) for d in range(1, n_ka)] + [s for s in SIDES if 0 not in s]
+    partners = [(d, 0) for d in range(1, n_gx)] + [(0, d) for d in range(1, n_ka)]
     for dx, dy in partners:
         pl.semaphore_signal(barrier, inc=1, device_id={"gx": gx_at(dx), "ka": ka_at(dy)}, device_id_type=MESH)
     pl.semaphore_wait(barrier, len(partners))
@@ -49,7 +53,8 @@
             device_id={"gx": gx_at(1)}, device_id_type=MESH)
         for m in range(M)
     ]
-    for c in halos:
+    early = 1
+    for c in halos[:early]:
         c.start()
 
     norm_msg[gx] = jnp.zeros((8, NZ), jnp.float32)
@@ -88,8 +93,11 @@
         return jnp.broadcast_to(jnp.sum(total, axis=1, keepdims=True), (8, NZ))
 
     norm_copies = exchange(norm_msg, norm_send, norm_recv)
-
-    perm_load.wait()
+    for c in halos[early:]:
+        c.start()
+
+    for c in [perm_load] + small_loads:
+        c.wait()
 
     def inverse_step(p, carry):
         inv[p] = 1.0 / perm[p]
@@ -109,8 +117,8 @@
         weight[m] = jnp.broadcast_to(sign * cells / norms[m:m + 1], (8, NZ))
 
     first_lane = lax.broadcasted_iota(jnp.int32, (R, NZ), 1) == 0
-    last_lane = lax.broadcasted_iota(jnp.int32, (W + R + W, NZ), 1) == NZ - 1
-    first_lane_wide = lax.broadcasted_iota(jnp.int32, (W + R + W, NZ), 1) == 0
+    last_lane = lax.broadcasted_iota(jnp.int32, (PLANES, W + R + W, NZ), 2) == NZ - 1
+    first_lane_wide = lax.broadcasted_iota(jnp.int32, (PLANES, W + R + W, NZ), 2) == 0
 
     def red_copy(p, c):
         return pltpu.make_async_remote_copy(
@@ -189,56 +197,63 @@
             total = total + recv[src, p]
         gpad[W + p, W:W + R] = total
 
-    def side_copies(stage, p0, planes):
+    def side_copies(stage, sides, p0, planes):
         copies = []
-        for i, (dx, dy) in enumerate(SIDES):
-            rows = R if dy == 0 else W
-            src_row = {0: W, 1: R, -1: W}[dy]
-            dst_row = {0: W, 1: 0, -1: W + R}[dy]
+        for i, (dx, dy, row, dst, rows) in enumerate(sides):
             copies.append(pltpu.make_async_remote_copy(
-                src_ref=gpad.at[pl.ds(W + p0, planes), pl.ds(src_row, rows)],
-                dst_ref=gpad.at[pl.ds(W - dx * PL + p0, planes), pl.ds(dst_row, rows)],
+                src_ref=gpad.at[pl.ds(W + p0, planes), pl.ds(row, rows)],
+                dst_ref=gpad.at[pl.ds(W - dx * PL + p0, planes), pl.ds(dst, rows)],
                 send_sem=side_send.at[stage, i], recv_sem=side_recv.at[stage, i],
                 device_id={"gx": gx_at(dx), "ka": ka_at(dy)}, device_id_type=MESH))
         for c in copies:
             c.start()
         return copies
 
+    faces = ((0, 1, R, 0, W), (0, -1, W, W + R, W), (1, 0, W, W, R), (-1, 0, W, W, R))
+    corners = tuple((dx, 0, row, row, W) for dx in (1, -1) for row in (0, W + R))
+
     def gather_step(p, carry):
         gathered(p)
         return carry
 
     lax.fori_loop(1, PL, gather_step, 0)
-    sides = side_copies(0, 1, PL - 1)
+    sides = side_copies(0, faces, 1, PL - 1)
     gathered(0)
-    sides += side_copies(1, 0, 1)
-    for c in sides:
+    sides += side_copies(1, faces, 0, 1)
+    for c in (sides[0], sides[1], sides[4], sides[5]):
         c.wait_recv()
+    last = side_copies(2, corners, 0, PL)
+    for c in sides[2:4] + sides[6:8] + last:
+        c.wait_recv()
+    sides += last
 
     scale = 1.0 / (1.0 + 6.0 * FILTER_WEIGHT)
+    rows_all = W + R + W
     for sweep in range(1, SWEEPS + 1):
-        source = gpad if sweep == 1 else dens.at[sweep % 2]
-        target = dens.at[(sweep + 1) % 2]
-
-        def relax(p, carry, sweep=sweep, source=source, target=target):
-            under, center = carry
-            over = source[p + 1]
-            near = under + over + pltpu.roll(center, 1, 0) + pltpu.roll(center, W + R + W - 1, 0)
-            near = near + jnp.where(first_lane_wide, 0.0, pltpu.roll(center, 1, 1))
-            near = near + jnp.where(last_lane, 0.0, pltpu.roll(center, NZ - 1, 1))
-            value = (gpad[p] + FILTER_WEIGHT * near) * scale
+        source = gpad if sweep == 1 else (dens_a, dens_b)[sweep % 2]
+        target = (dens_b, dens_a)[sweep % 2]
+        for p in range(sweep, 2 * W + PL - sweep, PLANES):
+            center = source[p:p + PLANES]
+            near = source[p - 1:p - 1 + PLANES] + source[p + 1:p + 1 + PLANES]
+            near = near + pltpu.roll(center, 1, 1) + pltpu.roll(center, rows_all - 1, 1)
+            near = near + jnp.where(first_lane_wide, 0.0, pltpu.roll(center, 1, 2))
+            near = near + jnp.where(last_lane, 0.0, pltpu.roll(center, NZ - 1, 2))
+            value = (gpad[p:p + PLANES] + FILTER_WEIGHT * near) * scale
             if sweep == SWEEPS:
-                out[p - W] = value[W:W + R]
+                out[p - W:p - W + PLANES] = value[:, W:W + R]
             else:
-                target[p] = value
-            return center, over
-
-        lax.fori_loop(sweep, 2 * W + PL - sweep, relax, (source[sweep - 1], source[sweep]))
+                target[p:p + PLANES] = value
+    out_copy = pltpu.make_async_copy(out, out_hbm, out_sem.at[0])
+    out_copy.start()
 
     energies = gather(energy_msg, energy_send, energy_recv)
     ratio = energies / norms
     for m in range(M):
         omega[m // B, m % B] = ratio[m, 0]
+    omega_copy = pltpu.make_async_copy(omega, omega_hbm, out_sem.at[1])
+    omega_copy.start()
+    out_copy.wait()
+    omega_copy.wait()
 
     for c in halos + norm_copies + energy_copies + sides:
         c.wait_send()
@@ -261,9 +276,8 @@
     return pl.pallas_call(
         functools.partial(kernel, n_gx, n_ka),
         out_shape=(jax.ShapeDtypeStruct((PL, R, NZ), f32), jax.ShapeDtypeStruct((K, B), f32)),
-        in_specs=[pl.BlockSpec(memory_space=pl.ANY), pl.BlockSpec(memory_space=pl.ANY),
-                  pl.BlockSpec(memory_space=pltpu.SMEM), pl.BlockSpec(memory_space=pltpu.SMEM)],
-        out_specs=(pl.BlockSpec(memory_space=pltpu.VMEM), pl.BlockSpec(memory_space=pltpu.SMEM)),
+        in_specs=[pl.BlockSpec(memory_space=pltpu.HBM)] * 4,
+        out_specs=(pl.BlockSpec(memory_space=pltpu.HBM), pl.BlockSpec(memory_space=pltpu.HBM)),
         scratch_shapes=[
             pltpu.VMEM((K, B, 2, 3, PL, NY, NZ), f32),
             pltpu.VMEM((K, B, 2, 2, NY, NZ), f32),
@@ -272,18 +286,23 @@
             pltpu.VMEM((n_ka, PL, R, NZ), f32),
             pltpu.VMEM((n_ka, PL, R, NZ), f32),
             pltpu.VMEM((PL + 2 * W, R + 2 * W, NZ), f32),
-            pltpu.VMEM((2, PL + 2 * W, R + 2 * W, NZ), f32),
+            pltpu.VMEM((PL + 2 * W, R + 2 * W, NZ), f32),
+            pltpu.VMEM((PL + 2 * W, R + 2 * W, NZ), f32),
+            pltpu.VMEM((PL, R, NZ), f32),
+            pltpu.SMEM((K, B), f32),
+            pltpu.SMEM((K,), f32),
+            pltpu.SMEM((K, B), jnp.int32),
             pltpu.VMEM((n_gx, 8, NZ), f32),
             pltpu.VMEM((n_gx, 8, NZ), f32),
             pltpu.VMEM((M, 8, NZ), f32),
             pltpu.VMEM((M, 8, NZ), f32),
             pltpu.VMEM((K, 2, 8, NZ), f32),
-            dma((M,)), dma, dma((M,)), dma((M,)),
+            dma((M,)), dma, dma((2,)), dma((2,)), dma((M,)), dma((M,)),
             dma((n_gx,)), dma((n_gx,)), dma((n_gx,)), dma((n_gx,)),
-            dma((n_ka, PL)), dma((n_ka, PL)), dma((2, len(SIDES))), dma((2, len(SIDES))),
+            dma((n_ka, PL)), dma((n_ka, PL)), dma((3, 4)), dma((3, 4)),
         ],
         compiler_params=pltpu.CompilerParams(
-            collective_id=0, has_side_effects=True, vmem_limit_bytes=48 * 1024 * 1024),
+            collective_id=0, has_side_effects=True, vmem_limit_bytes=62 * 1024 * 1024),
     )(bloch_modes, permittivity, bloch_phase, edge_side)
 
 

time: 55.5 us -> 37.7 us (0.68)
  Pallas kernels: 50.9 us -> 34.1 us
  local copies, waits for them, and re-layouts: 3.59 us -> 2.8 us
    pallas_call x1, Pallas kernels: 50.9 us -> 34.1 us  [shards(): pl.pallas_call(functools.partial(kernel, n_gx, n_ka), out_shape=(jax.Shap...]
    unnamed x8 -> x2, local copies, waits for them, and re-layouts: 3.59 us -> 2.8 us
where the time goes in v2:
time: 37.7 us; the launch traced here: 37.6 us
  Pallas kernels  34.1 us (90%)
  local copies, waits for them, and re-layouts  2.8 us (7%)
  between operations  0.64 us (2%)
    pallas_call x1, Pallas kernels, shards(): pl.pallas_call(functools.partial(kernel, n_gx, n_ka), out_shape=(jax.Shap...  34.1 us
    unnamed x2, local copies, waits for them, and re-layouts  2.8 us

profile of v2, /device:TPU:1, one launch (start us, length us, event | category | flops | bytes accessed | tf_op | source)
XLA Modules:
  0.0 37.6 jit_solution(1167587370045969646)
XLA Ops:
  0.6 34.1 %shard_map.59 = (f32[8,32,128]{2,1,0:T(8,128)}, f32[2,2]{1,0:T(2,128)}) custom-call(f32[2,2,2,3,8,128,128]{6,5,4,3,2,1,0:T(8,128)} %modes.1, f32[8,128,128]{2,1,0:T(8,128)} %perm_hbm.1, f32[2]{0:T(128)} %phase_hbm.1, s32[2,2]{1,0:T(2,128)} %edge_hbm.1), custom_call_target="tpu_custom_call" | custom-call | tf_op jit(solution)/shard_map/pallas_call | solution.py:276
  34.8 1.6 %copy.8 = f32[8,32,128]{2,1,0:T(8,128)} copy(f32[8,32,128]{2,1,0:T(8,128)} %get-tuple-element.4) | data formatting | bytes 262144
  36.4 1.2 %copy.9 = f32[2,2]{1,0:T(2,128)} copy(f32[2,2]{1,0:T(2,128)} %get-tuple-element.5) | data formatting | bytes 32

commit v3 on v2

--- a/solution.py
+++ b/solution.py
@@ -168,7 +168,7 @@
             red_copy(p, c).start()
 
     def stage_a(i, carry):
-        chunk(1 + i // n_ka, lax.rem(i, n_ka), False)
+        chunk(1 + i // n_ka, lax.rem(ka + 1 + i, n_ka), False)
         return carry
 
     lax.fori_loop(0, (PL - 1) * n_ka, stage_a, 0)
@@ -177,7 +177,7 @@
         c.wait_recv()
 
     def stage_b(c, carry):
-        chunk(0, c, True)
+        chunk(0, lax.rem(ka + 1 + c, n_ka), True)
         return carry
 
     lax.fori_loop(0, n_ka, stage_b, 0)
@@ -266,6 +266,13 @@
     lax.fori_loop(0, PL, sent, 0)
 
 
+def hand_over(density, omega, density_out, omega_out):
+    density_out[...] = density[...]
+    for k in range(omega.shape[0]):
+        for b in range(omega.shape[1]):
+            omega_out[k, b] = omega[k, b]
+
+
 def shards(n_gx, n_ka, bloch_modes, permittivity, bloch_phase, edge_side):
     K, B, _, _, PL, NY, NZ = bloch_modes.shape
     R = NY // n_ka
@@ -273,7 +280,7 @@
     M = K * B
     f32 = jnp.float32
     dma = pltpu.SemaphoreType.DMA
-    return pl.pallas_call(
+    held = pl.pallas_call(
         functools.partial(kernel, n_gx, n_ka),
         out_shape=(jax.ShapeDtypeStruct((PL, R, NZ), f32), jax.ShapeDtypeStruct((K, B), f32)),
         in_specs=[pl.BlockSpec(memory_space=pltpu.HBM)] * 4,
@@ -304,6 +311,12 @@
         compiler_params=pltpu.CompilerParams(
             collective_id=0, has_side_effects=True, vmem_limit_bytes=62 * 1024 * 1024),
     )(bloch_modes, permittivity, bloch_phase, edge_side)
+    return pl.pallas_call(
+        hand_over,
+        out_shape=(jax.ShapeDtypeStruct((PL, R, NZ), f32), jax.ShapeDtypeStruct((K, B), f32)),
+        in_specs=[pl.BlockSpec(memory_space=pltpu.VMEM), pl.BlockSpec(memory_space=pltpu.SMEM)],
+        out_specs=(pl.BlockSpec(memory_space=pltpu.VMEM), pl.BlockSpec(memory_space=pltpu.SMEM)),
+    )(*held)
 
 
 def solution(mesh):

time: 37.7 us -> 36.2 us (0.960)
  local copies, waits for them, and re-layouts: 2.8 us -> 0 us
  Pallas kernels: 34.1 us -> 35.4 us
    unnamed x2 -> x0, local copies, waits for them, and re-layouts: 2.8 us -> none
    pallas_call x0 -> x1, Pallas kernels: none -> 1.59 us  [shards(): pl.pallas_call(hand_over, out_shape=(jax.ShapeDtypeStruct((PL, R, NZ), f3...]
where the time goes in v3:
time: 36.2 us; the launch traced here: 36 us
  Pallas kernels  35.4 us (98%)
  between operations  0.64 us (2%)
    pallas_call x1, Pallas kernels, shards(): pl.pallas_call(functools.partial(kernel, n_gx, n_ka), out_shape=(jax.Shap...  33.8 us
    pallas_call x1, Pallas kernels, shards(): pl.pallas_call(hand_over, out_shape=(jax.ShapeDtypeStruct((PL, R, NZ), f3...  1.59 us

profile of v3, /device:TPU:1, one launch (start us, length us, event | category | flops | bytes accessed | tf_op | source)
XLA Modules:
  0.0 36.0 jit_solution(14415712196708640193)
XLA Ops:
  0.6 33.8 %shard_map.59 = (f32[8,32,128]{2,1,0:T(8,128)}, f32[2,2]{1,0:T(2,128)}) custom-call(f32[2,2,2,3,8,128,128]{6,5,4,3,2,1,0:T(8,128)} %modes.1, f32[8,128,128]{2,1,0:T(8,128)} %perm_hbm.1, f32[2]{0:T(128)} %phase_hbm.1, s32[2,2]{1,0:T(2,128)} %edge_hbm.1), custom_call_target="tpu_custom_call" | custom-call | tf_op jit(solution)/shard_map/pallas_call | solution.py:283
  34.4 1.6 %shard_map.60 = (f32[8,32,128]{2,1,0:T(8,128)}, f32[2,2]{1,0:T(2,128)}) custom-call(f32[8,32,128]{2,1,0:T(8,128)} %get-tuple-element.4.density, f32[2,2]{1,0:T(2,128)} %get-tuple-element.5.omega), custom_call_target="tpu_custom_call" | custom-call | tf_op jit(solution)/shard_map/pallas_call | solution.py:314

commit v4 on v3

--- a/solution.py
+++ b/solution.py
@@ -53,7 +53,7 @@
             device_id={"gx": gx_at(1)}, device_id_type=MESH)
         for m in range(M)
     ]
-    early = 1
+    early = 0
     for c in halos[:early]:
         c.start()
 

time: 36.2 us -> 36.5 us (level)
    pallas_call x1, Pallas kernels: 33.8 us -> 34.1 us  [shards(): pl.pallas_call(functools.partial(kernel, n_gx, n_ka), out_shape=(jax.Shap...]
where the time goes in v4:
time: 36.5 us; the launch traced here: 36.4 us
  Pallas kernels  35.7 us (98%)
  between operations  0.64 us (2%)
    pallas_call x1, Pallas kernels, shards(): pl.pallas_call(functools.partial(kernel, n_gx, n_ka), out_shape=(jax.Shap...  34.1 us
    pallas_call x1, Pallas kernels, shards(): pl.pallas_call(hand_over, out_shape=(jax.ShapeDtypeStruct((PL, R, NZ), f3...  1.59 us

profile of v4, /device:TPU:1, one launch (start us, length us, event | category | flops | bytes accessed | tf_op | source)
XLA Modules:
  0.0 36.4 jit_solution(8566954457952213269)
XLA Ops:
  0.6 34.1 %shard_map.59 = (f32[8,32,128]{2,1,0:T(8,128)}, f32[2,2]{1,0:T(2,128)}) custom-call(f32[2,2,2,3,8,128,128]{6,5,4,3,2,1,0:T(8,128)} %modes.1, f32[8,128,128]{2,1,0:T(8,128)} %perm_hbm.1, f32[2]{0:T(128)} %phase_hbm.1, s32[2,2]{1,0:T(2,128)} %edge_hbm.1), custom_call_target="tpu_custom_call" | custom-call | tf_op jit(solution)/shard_map/pallas_call | solution.py:283
  34.8 1.6 %shard_map.60 = (f32[8,32,128]{2,1,0:T(8,128)}, f32[2,2]{1,0:T(2,128)}) custom-call(f32[8,32,128]{2,1,0:T(8,128)} %get-tuple-element.4.density, f32[2,2]{1,0:T(2,128)} %get-tuple-element.5.omega), custom_call_target="tpu_custom_call" | custom-call | tf_op jit(solution)/shard_map/pallas_call | solution.py:314
